TPU v7x, 512 devices: a whole 4x4x16 slice. The times are simulated.
512 devices in a mesh: dp: 16 (over y, x), expert: 32 (over z, core).
Axes of the slice: x: 4, y: 4, z: 16, core: 2. Of those that a mesh axis runs over, the one named last changes fastest.
Arguments:
- cotangent: bfloat16 [65536, 2048], P(('dp', 'expert')), may hold values from -0.375 to 0.375
- routes: int32 [65536, 8], P(('dp', 'expert')), may hold values from 0 to 63, all different within a row; in each aligned block of 128 rows (0 to 127, 128 to 255, ...) at most 20 rows name the same one
- gate_weights: float32 [65536, 8], P(('dp', 'expert')), may hold values from 0.05 to 0.25
- hidden: bfloat16 [16, 64, 640, 768], P('dp', 'expert'), may hold values from -6 to 6
- galore_basis: bfloat16 [64, 768, 256], P('expert'), may hold values from -0.21875 to 0.21875
- moment: float32 [64, 256, 2048], P('expert', None, 'dp'), may hold values from -1.75 to 1.75
- second: float32 [64, 256, 2048], P('expert', None, 'dp'), may hold values from 0.01 to 1
Outputs:
- new_moment: float32 [64, 256, 2048], P('expert', None, 'dp')
- new_second: float32 [64, 256, 2048], P('expert', None, 'dp')
- update: float32 [64, 256, 2048], P('expert', None, 'dp')
Inputs may be any that keep to these rules, and one draw needn't show every extreme that they name: `routes`: in the rows of one device (128 aligned rows) no expert is named by more than 20 rows, a bound that some blocks reach.
All inputs are finite; a program needn't handle non-finite values.
Results may differ from a plain program's by a relative error of at most 0.0015.
Values may be sent and summed in bfloat16 or wider, within the bound.
A program may use at most 64 MiB of HBM per device.

v0:
```python
import jax
import jax.numpy as jnp
from jax import lax
from jax.sharding import PartitionSpec as P

STEP = 100


beta_one = 0.9
beta_two = 0.999
epsilon = 1e-08


def route_slots(flat_routes, experts):
    onehot = (flat_routes[:, None] == jnp.arange(experts, dtype=jnp.int32)[None, :]).astype(
        jnp.int32
    )
    before = jnp.cumsum(onehot, axis=0) - onehot
    return jnp.sum(before * onehot, axis=1)


def body(cotangent, routes, gate_weights, hidden, galore_basis, moment, second):
    route_count = routes.shape[1]
    senders = lax.axis_size("expert")
    local_experts = galore_basis.shape[0]
    experts = local_experts * senders
    capacity = hidden.shape[2] // senders
    feature_width = cotangent.shape[1]
    flat_routes = routes.reshape(-1)
    route_total = flat_routes.shape[0]
    target = flat_routes * capacity + route_slots(flat_routes, experts)
    source = jnp.full((experts * capacity,), route_total, jnp.int32)
    source = source.at[target].set(jnp.arange(route_total, dtype=jnp.int32))
    filled = source < route_total
    picked = jnp.minimum(source, route_total - 1)
    weight = jnp.where(filled, gate_weights.reshape(-1)[picked], 0.0)
    outgoing = (weight[:, None] * cotangent[picked // route_count].astype(jnp.float32)).astype(
        jnp.bfloat16
    )
    outgoing = outgoing.reshape(senders, local_experts * capacity, feature_width)
    arrived = lax.all_to_all(outgoing, "expert", split_axis=0, concat_axis=0, tiled=True)
    arrived = arrived.reshape(senders, local_experts, capacity, feature_width)
    projected = jnp.einsum(
        "jsf,jfr->jsr", hidden[0], galore_basis, preferred_element_type=jnp.float32
    ).astype(jnp.bfloat16)
    projected = projected.reshape(local_experts, senders, capacity, projected.shape[2])
    partial_value = jnp.einsum(
        "jscr,sjcd->jrd", projected, arrived, preferred_element_type=jnp.float32
    )
    share_cols = moment.shape[2]
    summed = lax.psum(partial_value, "dp")
    gradient = lax.dynamic_slice_in_dim(summed, lax.axis_index("dp") * share_cols, share_cols, 2)
    new_moment = beta_one * moment + (1.0 - beta_one) * gradient
    new_second = beta_two * second + (1.0 - beta_two) * gradient * gradient
    update = (
        new_moment
        / (1.0 - beta_one**STEP)
        / (jnp.sqrt(new_second / (1.0 - beta_two**STEP)) + epsilon)
    )
    return (new_moment, new_second, update)


def solution(mesh):
    placed = (
        P(("dp", "expert"), None),
        P(("dp", "expert"), None),
        P(("dp", "expert"), None),
        P("dp", "expert", None, None),
        P("expert", None, None),
        P("expert", None, "dp"),
        P("expert", None, "dp"),
    )
    return jax.shard_map(
        body,
        mesh=mesh,
        in_specs=placed,
        out_specs=(P("expert", None, "dp"), P("expert", None, "dp"), P("expert", None, "dp")),
        check_vma=False,
    )
```

profile of v0, /device:TPU:1, one launch (start us, length us, event | category | flops | bytes accessed | tf_op | source)
XLA Modules:
  0.0 446.4 jit_solution(15603314482128951789)
XLA Ops:
  7.2 0.0 copy-start
  7.2 0.9 copy.24
  8.1 0.1 eq.29
  8.2 0.1 eq.25
  8.3 0.7 broadcast_multiply_fusion
  9.0 18.0 %reduce-window.6 = s32[64,8,128]{2,1,0:T(8,128)S(1)} reduce-window(s32[64,8,128]{2,1,0:T(8,128)S(1)} %fusion.11, s32[]{:T(128)} %constant.24.clone.1), window={size=1x1x128 pad=0_0x0_0x127_0}, to_apply=%region_0.0 | reduce-window | flops 8323072 | bytes 524292 | tf_op jit(solution)/shard_map/reduce-window
  27.0 0.0 copy-start.1
  27.0 0.1 slice.12
  27.2 0.1 copy.26
  27.3 0.1 copy.27
  27.4 0.1 broadcast_add_fusion
  27.6 0.1 copy.23
  27.7 0.1 mul.64
  27.8 0.1 fusion.10
  27.9 4.3 scatter_custom_fusion
  32.2 0.8 copy.28
  33.0 0.1 reshape.73
  33.1 5.0 %gather_fusion = f32[1280]{0:T(1024)S(1)} fusion(f32[1024]{0:T(1024)S(1)} %reshape.73, s32[2048]{0:T(1024)S(1)} %get-tuple-element.9), kind=kCustom, calls=%fused_computation | custom fusion | bytes 15360 | tf_op jit(solution)/shard_map/gather | solution.py:36
  38.1 0.1 mul.66
  38.2 0.0 copy-done.1
  38.2 6.1 %gather_fusion.1 = bf16[1280,2048]{1,0:T(8,128)(2,1)} fusion(bf16[128,2048]{1,0:T(8,128)(2,1)S(1)} %copy-done.1, s32[2048]{0:T(1024)S(1)} %get-tuple-element.8), kind=kCustom, calls=%fused_computation.1 | custom fusion | bytes 10490880 | tf_op jit(solution)/shard_map/gather | solution.py:37
  44.3 5.7 %fusion = bf16[32,40,2048]{2,1,0:T(8,128)(2,1)} fusion(bf16[32,40,2048]{2,1,0:T(8,128)(2,1)} %bitcast.34, f32[32,40]{1,0:T(8,128)S(1)} %mul.66), kind=kLoop, calls=%fused_computation.4 | loop fusion | flops 7864320 | bytes 10490880 | tf_op jit(solution)/shard_map/convert_element_type | solution.py:37
  50.0 0.0 copy-start.4
  50.0 16.9 %all-to-all-start = ((bf16[32,40,2048]{2,1,0:T(8,128)(2,1)}), bf16[32,40,2048]{2,1,0:T(8,128)(2,1)}, u32[]{:S(2)}, u32[]{:S(2)}) async-start(bf16[32,40,2048]{2,1,0:T(8,128)(2,1)} %fusion), calls=%async_computation | async-start | bytes 10485760 | tf_op jit(solution)/shard_map/all_to_all | solution.py:41
  67.0 0.0 all-reduce.2.cloned.1.call-start
  67.0 0.0 copy-done
  67.0 0.0 copy-done.4
  67.1 0.7 fusion.3
  67.7 0.7 copy.22
  68.4 230.4 %all-to-all-done = bf16[32,40,2048]{2,1,0:T(8,128)(2,1)} async-done(((bf16[32,40,2048]{2,1,0:T(8,128)(2,1)}), bf16[32,40,2048]{2,1,0:T(8,128)(2,1)}, u32[]{:S(2)}, u32[]{:S(2)}) %all-to-all-start) | async-done | bytes 5242912 | tf_op jit(solution)/shard_map/all_to_all | solution.py:41
  298.8 5.4 %copy.29 = bf16[32,40,2048]{2,0,1:T(8,128)(2,1)S(1)} copy(bf16[32,40,2048]{2,1,0:T(8,128)(2,1)} %all-to-all-done) | data formatting | bytes 10485760 | tf_op jit(solution)/shard_map/all_to_all | solution.py:41
  304.2 0.0 copy-start.2
  304.2 0.0 copy-start.3
  304.2 3.8 convolution_bitcast_fusion
  308.0 0.0 all-reduce.2.cloned.1.call-update
  308.0 129.6 %all-reduce.2.cloned.1.call-done = f32[2,256,2048]{2,1,0:T(8,128)} async-done(((f32[2,256,2048]{2,1,0:T(8,128)}), f32[2,256,2048]{2,1,0:T(8,128)}) %all-reduce.2.cloned.1.call-update) | async-done | bytes 4194320 | tf_op jit(solution)/shard_map/psum | solution.py:51
  437.6 0.0 copy-done.2
  437.6 0.0 copy-done.3
  437.6 1.9 add_divide_fusion
  (8 shorter events, 0.1 us)
Async XLA Ops:
  7.2 59.9 %copy-start = (bf16[1,2,640,768]{3,2,1,0:T(8,128)(2,1)S(1)}, bf16[1,2,640,768]{3,2,1,0:T(8,128)(2,1)}, u32[]{:S(2)}) copy-start(bf16[1,2,640,768]{3,2,1,0:T(8,128)(2,1)} %param.10) | copy-start | bytes 5898244
  27.0 11.2 %copy-start.1 = (bf16[128,2048]{1,0:T(8,128)(2,1)S(1)}, bf16[128,2048]{1,0:T(8,128)(2,1)}, u32[]{:S(2)}) copy-start(bf16[128,2048]{1,0:T(8,128)(2,1)} %param.7) | copy-start | bytes 1572868
  50.0 17.0 %copy-start.4 = (bf16[2,768,256]{2,1,0:T(8,128)(2,1)S(1)}, bf16[2,768,256]{2,1,0:T(8,128)(2,1)}, u32[]{:S(2)}) copy-start(bf16[2,768,256]{2,1,0:T(8,128)(2,1)} %param.11) | copy-start | bytes 2359300
  50.0 248.8 %all-to-all-start = ((bf16[32,40,2048]{2,1,0:T(8,128)(2,1)}), bf16[32,40,2048]{2,1,0:T(8,128)(2,1)}, u32[]{:S(2)}, u32[]{:S(2)}) async-start(bf16[32,40,2048]{2,1,0:T(8,128)(2,1)} %fusion), calls=%async_computation | async-start | bytes 10485760 | tf_op jit(solution)/shard_map/all_to_all | solution.py:41
  67.0 370.6 %all-reduce.2.cloned.1.call-start = ((), (), s32[]{:S(2)}) async-start(), calls=%async_computation.1 | async-start | bytes 8388608 | tf_op jit(solution)/shard_map/psum | solution.py:51
  304.2 133.4 %copy-start.2 = (f32[2,256,128]{2,1,0:T(8,128)S(1)}, f32[2,256,128]{2,1,0:T(8,128)}, u32[]{:S(2)}) copy-start(f32[2,256,128]{2,1,0:T(8,128)} %param.13) | copy-start | bytes 786436
  304.2 133.4 %copy-start.3 = (f32[2,256,128]{2,1,0:T(8,128)S(1)}, f32[2,256,128]{2,1,0:T(8,128)}, u32[]{:S(2)}) copy-start(f32[2,256,128]{2,1,0:T(8,128)} %param.12) | copy-start | bytes 786436
Sparse Core Ops, SparseCore 0:
  308.1 129.3 all-reduce.1
where the time goes:
time: 447 us; the launch traced here: 446 us
  waiting for transfers between devices  360 us (81%)
  other arithmetic  26.6 us (6%)
  local copies, waits for them, and re-layouts  24.1 us (5%)
  starting transfers between devices  17 us (4%)
  between operations  14.2 us (3%)
  matrix products  4.49 us (1%)
    all_to_all x1, waiting for transfers between devices, body(): lax.all_to_all(outgoing, 'expert', split_axis=0, concat_axis=0, tiled=True)  230 us
    psum x1, waiting for transfers between devices, body(): summed = lax.psum(partial_value, 'dp')  130 us
    another operation x3, other arithmetic  18.2 us
    all_to_all x1, starting transfers between devices, body(): lax.all_to_all(outgoing, 'expert', split_axis=0, concat_axis=0, tiled=True)  16.9 us
  transfers between devices with their start and end apart: 2, of which 2 were waited for; matrix products, arithmetic and copies ran while one was open for 0% of the time, Pallas kernels for 0%

commit v1 on v0

v1 whole, which is shorter than its diff:
```python
import jax
import jax.numpy as jnp
from jax import lax
from jax.sharding import PartitionSpec as P

STEP = 100


beta_one = 0.9
beta_two = 0.999
epsilon = 1e-08


def body(cotangent, routes, gate_weights, hidden, galore_basis, moment, second):
    senders = lax.axis_size("expert")
    local_experts = galore_basis.shape[0]
    capacity = hidden.shape[2] // senders
    tokens, feature_width = cotangent.shape
    me = lax.axis_index("expert")
    gathered = lax.all_gather(cotangent, "expert", axis=0)
    all_routes = lax.all_gather(routes, "expert", axis=0)
    all_gates = lax.all_gather(gate_weights, "expert", axis=0)
    projected = jnp.einsum(
        "jsf,jfr->jsr", hidden[0], galore_basis, preferred_element_type=jnp.float32
    ).astype(jnp.bfloat16)
    projected = projected.reshape(local_experts, senders, capacity, projected.shape[2])
    mine = me * local_experts + jnp.arange(local_experts, dtype=jnp.int32)
    named = all_routes[None] == mine[:, None, None, None]
    hit = jnp.any(named, axis=3)
    weight = jnp.sum(jnp.where(named, all_gates[None], 0.0), axis=3)
    earlier = jnp.tril(jnp.ones((tokens, tokens), jnp.bfloat16), -1)
    slot = jnp.einsum(
        "jsu,tu->jst", hit.astype(jnp.bfloat16), earlier, preferred_element_type=jnp.float32
    ).astype(jnp.int32)
    chosen = hit[:, :, None, :] & (
        slot[:, :, None, :] == jnp.arange(capacity, dtype=jnp.int32)[None, None, :, None]
    )
    row_weight = jnp.sum(jnp.where(chosen, weight[:, :, None, :], 0.0), axis=3)
    rows = jnp.einsum(
        "jsct,std->jscd", chosen.astype(jnp.bfloat16), gathered, preferred_element_type=jnp.float32
    )
    table = (row_weight[..., None] * rows).astype(jnp.bfloat16)
    partial_value = jnp.einsum("jscr,jscd->jrd", projected, table, preferred_element_type=jnp.float32)
    gradient = lax.psum_scatter(partial_value, "dp", scatter_dimension=2, tiled=True)
    new_moment = beta_one * moment + (1.0 - beta_one) * gradient
    new_second = beta_two * second + (1.0 - beta_two) * gradient * gradient
    update = (
        new_moment
        / (1.0 - beta_one**STEP)
        / (jnp.sqrt(new_second / (1.0 - beta_two**STEP)) + epsilon)
    )
    return (new_moment, new_second, update)


def solution(mesh):
    placed = (
        P(("dp", "expert"), None),
        P(("dp", "expert"), None),
        P(("dp", "expert"), None),
        P("dp", "expert", None, None),
        P("expert", None, None),
        P("expert", None, "dp"),
        P("expert", None, "dp"),
    )
    return jax.shard_map(
        body,
        mesh=mesh,
        in_specs=placed,
        out_specs=(P("expert", None, "dp"), P("expert", None, "dp"), P("expert", None, "dp")),
        check_vma=False,
    )
```

time: 447 us -> 234 us (0.52)
  waiting for transfers between devices: 360 us -> 135 us
  blocking collectives: 0 us -> 66.3 us
  other arithmetic: 26.6 us -> 2.61 us
  local copies, waits for them, and re-layouts: 24.1 us -> 0.8 us
  starting transfers between devices: 17 us -> 0.08 us
  matrix products: 4.49 us -> 13.9 us
    all_to_all x1 -> x0, waiting for transfers between devices: 230 us -> none  [body(): lax.all_to_all(outgoing, 'expert', split_axis=0, concat_axis=0, tiled=True)]
    psum x1 -> x0, waiting for transfers between devices: 130 us -> none  [body(): summed = lax.psum(partial_value, 'dp')]
    reduce_scatter x0 -> x1, waiting for transfers between devices: none -> 88.8 us  [body(): lax.psum_scatter(partial_value, 'dp', scatter_dimension=2, tiled=True)]
    all_gather x0 -> x2, blocking collectives: none -> 66.3 us  [the longest x1 38.4 us: body(): all_routes = lax.all_gather(routes, 'expert', axis=0)]
    all_gather x0 -> x1, waiting for transfers between devices: none -> 45.8 us  [body(): gathered = lax.all_gather(cotangent, 'expert', axis=0)]
    another operation x3 -> x0, other arithmetic: 18.2 us -> none
    all_to_all x1 -> x0, starting transfers between devices: 16.9 us -> none  [body(): lax.all_to_all(outgoing, 'expert', split_axis=0, concat_axis=0, tiled=True)]
    gather x2 -> x0, local copies, waits for them, and re-layouts: 11.1 us -> none  [the longest x1 6.13 us: body(): cotangent[picked // route_count].astype(jnp.float32)]
  transfers between devices with their start and end apart: 2 -> 2, of which waited for: 2 -> 2; matrix products, arithmetic and copies ran while one was open for 0% -> 1% of each run, Pallas kernels for 0% -> 0%
where the time goes in v1:
time: 234 us; the launch traced here: 233 us
  waiting for transfers between devices  135 us (58%)
  blocking collectives  66.3 us (28%)
  between operations  14.1 us (6%)
  matrix products  13.9 us (6%)
  other arithmetic  2.61 us (1%)
    reduce_scatter x1, waiting for transfers between devices, body(): lax.psum_scatter(partial_value, 'dp', scatter_dimension=2, tiled=True)  88.8 us
    all_gather x1, waiting for transfers between devices, body(): gathered = lax.all_gather(cotangent, 'expert', axis=0)  45.8 us
    all_gather x1, blocking collectives, body(): all_routes = lax.all_gather(routes, 'expert', axis=0)  38.4 us
    all_gather x1, blocking collectives, body(): all_gates = lax.all_gather(gate_weights, 'expert', axis=0)  27.9 us
    dot_general x1, matrix products, body(): jnp.einsum('jsct,std->jscd', chosen.astype(jnp.bfloat16), gathered, prefe...  8.09 us
  transfers between devices with their start and end apart: 2, of which 2 were waited for; matrix products, arithmetic and copies ran while one was open for 1% of the time, Pallas kernels for 0%

profile of v1, /device:TPU:1, one launch (start us, length us, event | category | flops | bytes accessed | tf_op | source)
XLA Modules:
  0.0 233.1 jit_solution(12435347311671960373)
XLA Ops:
  7.2 0.0 copy-start
  7.2 0.0 all-gather.5.cloned.1.call-start
  7.2 0.7 all-gather.5.cloned.1.call-update
  7.9 0.0 reduce-scatter.2.cloned.1.call-start
  8.0 38.4 %all-gather = s32[4096,8]{0,1:T(8,128)S(1)} all-gather(s32[128,8]{0,1:T(8,128)} %param.8), channel_id=2, replica_groups=mesh['dp'=16,'expert'=32] {'expert'}, dimensions={0}, use_global_device_ids=true | all-gather | bytes 135168 | tf_op jit(solution)/shard_map/all_gather | solution.py:21
  46.3 27.9 %all-gather.1 = f32[4096,8]{0,1:T(8,128)S(1)} all-gather(f32[128,8]{0,1:T(8,128)} %param.9), channel_id=3, replica_groups=mesh['dp'=16,'expert'=32] {'expert'}, dimensions={0}, use_global_device_ids=true | all-gather | bytes 135168 | tf_op jit(solution)/shard_map/all_gather | solution.py:22
  74.3 0.2 compare_reduce_fusion
  74.4 0.1 fusion.14
  74.6 0.2 convolution_convert_fusion
  74.8 0.3 select_reduce_fusion
  75.0 0.1 copy.18
  75.1 0.0 copy-done
  75.2 1.8 fusion.8
  77.0 0.7 copy.17
  77.6 0.1 fusion.13
  77.8 45.8 %all-gather.5.cloned.1.call-done = bf16[4096,2048]{1,0:T(8,128)(2,1)} async-done(((bf16[128,2048]{1,0:T(8,128)(2,1)}), bf16[4096,2048]{1,0:T(8,128)(2,1)}) %all-gather.5.cloned.1.call-update) | async-done | bytes 16777232 | tf_op jit(solution)/shard_map/all_gather | solution.py:20
  123.6 8.1 %fusion = bf16[2,32,20,2048]{3,2,0,1:T(8,128)(2,1)S(1)} fusion(f32[2,32,20]{2,0,1:T(2,128)S(1)} %copy.18, bf16[32,128,2048,1]{2,1,3,0:T(8,128)(2,1)} %bitcast.26, pred[2,32,20,128]{3,1,2,0:T(32,128)(4,1)S(1)} %fusion.13), kind=kOutput, calls=%fused_computation.1 | convolution fusion | flops 676331520 | bytes 22189056 | tf_op jit(solution)/shard_map/jsct,std->jscd/dot_general | solution.py:39
  131.7 0.0 copy-start.1
  131.7 0.0 copy-start.2
  131.7 3.8 %fusion.3 = f32[2,256,2048]{2,1,0:T(8,128)} fusion(bf16[2,32,20,2048]{3,2,0,1:T(8,128)(2,1)S(1)} %fusion, bf16[2,32,20,256]{3,0,2,1:T(2,128)(2,1)S(1)} %bitcast.29), kind=kOutput, calls=%fused_computation.4 | convolution fusion | flops 1342177280 | bytes 10092544 | tf_op jit(solution)/shard_map/jscr,jscd->jrd/dot_general | solution.py:43
  135.5 0.0 reduce-scatter.2.cloned.1.call-update
  135.6 88.8 %reduce-scatter.2.cloned.1.call-done = f32[2,256,128]{2,1,0:T(8,128)} async-done(((f32[2,256,2048]{2,1,0:T(8,128)}), f32[2,256,128]{2,1,0:T(8,128)}) %reduce-scatter.2.cloned.1.call-update) | async-done | bytes 262160 | tf_op jit(solution)/shard_map/reduce_scatter | solution.py:44
  224.4 0.0 copy-done.1
  224.4 0.0 copy-done.2
  224.4 1.9 add_divide_fusion
  (2 shorter events, 0.0 us)
Async XLA Ops:
  7.2 68.0 %copy-start = (bf16[1,2,640,768]{3,2,1,0:T(8,128)(2,1)S(1)}, bf16[1,2,640,768]{3,2,1,0:T(8,128)(2,1)}, u32[]{:S(2)}) copy-start(bf16[1,2,640,768]{3,2,1,0:T(8,128)(2,1)} %param.10) | copy-start | bytes 5898244
  7.2 116.4 %all-gather.5.cloned.1.call-start = ((), (), s32[]{:S(2)}) async-start(), calls=%async_computation.2 | async-start | bytes 17301504 | tf_op jit(solution)/shard_map/all_gather | solution.py:20
  7.9 216.5 %reduce-scatter.2.cloned.1.call-start = ((), (), s32[]{:S(2)}) async-start(), calls=%async_computation.1 | async-start | bytes 4456448 | tf_op jit(solution)/shard_map/reduce_scatter | solution.py:44
  131.7 92.7 %copy-start.1 = (f32[2,256,128]{2,1,0:T(8,128)S(1)}, f32[2,256,128]{2,1,0:T(8,128)}, u32[]{:S(2)}) copy-start(f32[2,256,128]{2,1,0:T(8,128)} %param.13) | copy-start | bytes 786436
  131.7 92.7 %copy-start.2 = (f32[2,256,128]{2,1,0:T(8,128)S(1)}, f32[2,256,128]{2,1,0:T(8,128)}, u32[]{:S(2)}) copy-start(f32[2,256,128]{2,1,0:T(8,128)} %param.12) | copy-start | bytes 786436
Sparse Core Ops, SparseCore 0:
  10.1 113.4 all-gather.4
  135.7 88.6 reduce-scatter.1

commit v2 on v1

v2 whole, which is shorter than its diff:
```python
import functools

import jax
import jax.numpy as jnp
from jax import lax
from jax.experimental import pallas as pl
from jax.experimental.pallas import tpu as pltpu
from jax.sharding import PartitionSpec as P

STEP = 100
MESH = pl.DeviceIdType.MESH

beta_one = 0.9
beta_two = 0.999
epsilon = 1e-08

NX = 4
NZ = 16
PLANE = NX * NX
HALF = 8
CAP = 20
PAIR = 2 * CAP
R = 256
LANE = 128
TOK = 128
WIDE = NX * LANE
FULL = 32767.0


def landed(ref, sem):
    pltpu.make_async_copy(ref, ref, sem).wait()


def kernel(
    cx, aux, pz, out,
    prx, pg, crx, arx, tab, gacc, rxq, rxs, txq, txs, finq, fins,
    z_send, prx_sem, c_send, a_send, c_recv, a_recv,
    sc_send, sa_send, sc_recv, sa_recv, p_send, p_recv,
    q_send, s_send, q_recv, s_recv, fq_send, fs_send, fq_recv, fs_recv,
):
    dp = lax.axis_index("dp")
    ex = lax.axis_index("expert")
    x, y = lax.rem(dp, NX), dp // NX
    z, k = ex // 2, lax.rem(ex, 2)
    sibling = z * 2 + 1 - k

    def push(src, dst, send, recv, device):
        pltpu.make_async_remote_copy(
            src_ref=src, dst_ref=dst, send_sem=send, recv_sem=recv, device_id=device, device_id_type=MESH
        ).start()

    mine = pl.ds(k * 2, 2)
    for d in range(HALF, 0, -1):
        down = lax.rem(z - d + NZ, NZ)
        push(pz.at[down], prx.at[HALF - d, mine], z_send.at[HALF - d], prx_sem.at[HALF - d, k], (dp, down * 2))
        if d < HALF:
            up = lax.rem(z + d, NZ)
            push(pz.at[up], prx.at[HALF - 1 - d, mine], z_send.at[HALF + d], prx_sem.at[HALF - 1 - d, k], (dp, up * 2 + 1))

    @pl.when(k == 0)
    def _():
        push(pz.at[z], prx.at[HALF - 1, mine], z_send.at[HALF], prx_sem.at[HALF - 1, k], (dp, sibling))

    @pl.when(k == 1)
    def _():
        pltpu.make_async_copy(pz.at[z], prx.at[HALF - 1, mine], prx_sem.at[HALF - 1, k]).start()

    pltpu.make_async_copy(cx.at[x], crx.at[dp, k], c_recv.at[dp]).start()
    pltpu.make_async_copy(aux.at[y], arx.at[dp, k], a_recv.at[dp]).start()

    def scatter(o, carry):
        to = lax.rem(dp + o, PLANE)
        push(aux.at[to // NX], arx.at[dp, k], a_send.at[o], a_recv.at[dp], (to, ex))
        push(cx.at[lax.rem(to, NX)], crx.at[dp, k], c_send.at[o], c_recv.at[dp], (to, ex))
        return carry

    lax.fori_loop(1, PLANE, scatter, 0)

    def spread(i):
        for core in range(2):
            landed(prx.at[i, pl.ds(core * 2, 2)], prx_sem.at[i, core])
        pltpu.make_async_copy(prx.at[i, y], pg.at[i, dp], p_recv.at[i]).start()

        def one(o, carry):
            to = lax.rem(dp + o, PLANE)
            push(prx.at[i, to // NX], pg.at[i, dp], p_send.at[i], p_recv.at[i], (to, ex))
            return carry

        lax.fori_loop(1, PLANE, one, 0)

    def share(o, carry):
        source = lax.rem(dp - o + PLANE, PLANE)
        landed(arx.at[source, k], a_recv.at[source])
        push(arx.at[source, k], arx.at[source, k], sa_send.at[source], sa_recv.at[source], (dp, sibling))
        landed(crx.at[source, k], c_recv.at[source])
        push(crx.at[source, k], crx.at[source, k], sc_send.at[source], sc_recv.at[source], (dp, sibling))
        return carry

    lax.fori_loop(0, 5, share, 0)
    spread(0)
    lax.fori_loop(5, 9, share, 0)
    spread(1)
    lax.fori_loop(9, 13, share, 0)
    spread(2)
    lax.fori_loop(13, PLANE, share, 0)

    first = pl.multiple_of((1 - k) * HALF, HALF)
    slot = lax.broadcasted_iota(jnp.int32, (HALF, PAIR, 2 * TOK), 1).astype(jnp.float32)

    def rows_of(r):
        landed(arx.at[r, 1 - k], sa_recv.at[r])
        landed(crx.at[r, 1 - k], sc_recv.at[r])
        place = jnp.concatenate([arx[r, c, 0, pl.ds(first, HALF), :] for c in range(2)], axis=1)
        gate = jnp.concatenate([arx[r, c, 1, pl.ds(first, HALF), :] for c in range(2)], axis=1)
        here = slot == place[:, None, :]
        weight = jnp.sum(jnp.where(here, gate[:, None, :], 0.0), axis=2, keepdims=True)
        pick = jnp.where(here, 1.0, 0.0).reshape(HALF * PAIR, 2 * TOK).astype(jnp.bfloat16)
        rows = jnp.dot(pick, crx[r].reshape(2 * TOK, WIDE), preferred_element_type=jnp.float32)
        return rows.reshape(HALF, PAIR, WIDE) * weight

    def build(pair, carry):
        both = jnp.concatenate([rows_of(2 * pair), rows_of(2 * pair + 1)], axis=1)
        tab[:, pair] = both.astype(jnp.bfloat16)
        return carry

    lax.fori_loop(0, PLANE // 2, build, 0)

    onward = lax.rem(z + 1 - 2 * k + NZ, NZ) * 2 + k

    def contribution(i):
        landed(pg.at[i], p_recv.at[i])
        got = pg[i].astype(jnp.float32).reshape(PLANE, 2, PAIR, LANE)
        projected = jnp.concatenate([got[:, h].reshape(PLANE * PAIR, LANE) for h in range(2)], axis=1)
        table = tab[jnp.where(k == 0, HALF - 1 - i, i)].reshape(PLANE * PAIR, WIDE)
        gacc[...] = lax.dot_general(
            projected.astype(jnp.bfloat16), table, (((0,), (0,)), ((), ())), preferred_element_type=jnp.float32
        )

    def arrived(i, b):
        landed(rxs.at[i, b], s_recv.at[i, b])
        landed(rxq.at[i, b], q_recv.at[i, b])
        return rxq[i, b].astype(jnp.int32).astype(jnp.float32) * rxs[i, b, 0:1, :]

    def code(value, i, b):
        most = jnp.maximum(jnp.max(jnp.abs(value), axis=0, keepdims=True), 1e-33)
        txq[i, b] = jnp.round(value * (FULL / most)).astype(jnp.int32).astype(jnp.int16)
        txs[i, b] = jnp.broadcast_to(most * (1.0 / FULL), (8, LANE))

    def block(b):
        return gacc[:, b * LANE : (b + 1) * LANE]

    def send_on(value, i, b):
        code(value, i, b)
        push(txs.at[i, b], rxs.at[i + 1, b], s_send.at[i, b], s_recv.at[i + 1, b], (dp, onward))
        push(txq.at[i, b], rxq.at[i + 1, b], q_send.at[i, b], q_recv.at[i + 1, b], (dp, onward))

    for i in range(HALF - 1):
        if i + 3 < HALF:
            spread(i + 3)
        contribution(i)
        for b in range(NX):
            send_on(block(b) if i == 0 else block(b) + arrived(i, b), i, b)
    contribution(HALF - 1)

    owner_core = y // 2
    owner = z * 2 + owner_core
    part = lax.rem(y, 2)

    def finish(value, b):
        code(value, HALF, b)
        here = (y == b) & (owner_core == k)
        to = b * NX + x

        @pl.when(here)
        def _():
            pltpu.make_async_copy(txs.at[HALF, b], fins.at[k, part], fs_recv.at[k, part]).start()
            pltpu.make_async_copy(txq.at[HALF, b], finq.at[k, part], fq_recv.at[k, part]).start()

        @pl.when(jnp.logical_not(here))
        def _():
            push(txs.at[HALF, b], fins.at[k, part], fs_send.at[b], fs_recv.at[k, part], (to, owner))
            push(txq.at[HALF, b], finq.at[k, part], fq_send.at[b], fq_recv.at[k, part], (to, owner))

    @pl.when(k == 0)
    def _():
        for b in range(NX):
            send_on(block(b) + arrived(HALF - 1, b), HALF - 1, b)
        for b in range(NX):
            finish(arrived(HALF, b), b)

    @pl.when(k == 1)
    def _():
        for b in range(NX):
            finish(block(b) + arrived(HALF - 1, b), b)

    for j in range(2):
        total = None
        for core in range(2):
            landed(fins.at[core, j], fs_recv.at[core, j])
            landed(finq.at[core, j], fq_recv.at[core, j])
            value = finq[core, j].astype(jnp.int32).astype(jnp.float32) * fins[core, j, 0:1, :]
            total = value if total is None else total + value
        out[j] = total

    for i in range(HALF):
        landed(pz.at[0], z_send.at[i])
        if i > 0:
            landed(pz.at[0], z_send.at[HALF + i])
        landed(pg.at[i, pl.ds(0, PLANE - 1)], p_send.at[i])

    @pl.when(k == 0)
    def _():
        landed(pz.at[0], z_send.at[HALF])

    def left(o, carry):
        landed(aux.at[0], a_send.at[o])
        landed(cx.at[0], c_send.at[o])
        return carry

    lax.fori_loop(1, PLANE, left, 0)

    def shared(o, carry):
        landed(aux.at[0], sa_send.at[o])
        landed(cx.at[0], sc_send.at[o])
        return carry

    lax.fori_loop(0, PLANE, shared, 0)

    def sent(i):
        for b in range(NX):
            landed(txs.at[i, b], s_send.at[i, b])
            landed(txq.at[i, b], q_send.at[i, b])

    for i in range(HALF - 1):
        sent(i)

    @pl.when(k == 0)
    def _():
        sent(HALF - 1)

    for b in range(NX):

        @pl.when(jnp.logical_not((y == b) & (owner_core == k)))
        def _():
            landed(txs.at[HALF, b], fs_send.at[b])
            landed(txq.at[HALF, b], fq_send.at[b])


def exchange(cx, aux, pz):
    dma = pltpu.SemaphoreType.DMA
    return pl.pallas_call(
        kernel,
        out_shape=jax.ShapeDtypeStruct((2, R, LANE), jnp.float32),
        in_specs=[pl.BlockSpec(memory_space=pltpu.VMEM)] * 3,
        out_specs=pl.BlockSpec(memory_space=pltpu.VMEM),
        scratch_shapes=[
            pltpu.VMEM((HALF, NX, 2 * PAIR, LANE), jnp.bfloat16),
            pltpu.VMEM((HALF, PLANE, 2 * PAIR, LANE), jnp.bfloat16),
            pltpu.VMEM((PLANE, 2, TOK, WIDE), jnp.bfloat16),
            pltpu.VMEM((PLANE, 2, 2, NZ, TOK), jnp.float32),
            pltpu.VMEM((HALF, PLANE // 2, 2 * PAIR, WIDE), jnp.bfloat16),
            pltpu.VMEM((R, WIDE), jnp.float32),
            pltpu.VMEM((HALF + 1, NX, R, LANE), jnp.int16),
            pltpu.VMEM((HALF + 1, NX, 8, LANE), jnp.float32),
            pltpu.VMEM((HALF + 1, NX, R, LANE), jnp.int16),
            pltpu.VMEM((HALF + 1, NX, 8, LANE), jnp.float32),
            pltpu.VMEM((2, 2, R, LANE), jnp.int16),
            pltpu.VMEM((2, 2, 8, LANE), jnp.float32),
            dma((2 * HALF,)),
            dma((HALF, 2)),
            dma((PLANE,)), dma((PLANE,)), dma((PLANE,)), dma((PLANE,)),
            dma((PLANE,)), dma((PLANE,)), dma((PLANE,)), dma((PLANE,)),
            dma((HALF,)), dma((HALF,)),
            dma((HALF, NX)), dma((HALF, NX)),
            dma((HALF + 1, NX)), dma((HALF + 1, NX)),
            dma((NX,)), dma((NX,)),
            dma((2, 2)), dma((2, 2)),
        ],
        compiler_params=pltpu.CompilerParams(has_side_effects=True, vmem_limit_bytes=48 * 1024 * 1024),
        cost_estimate=pl.CostEstimate(flops=2_700_000_000, bytes_accessed=4_000_000, transcendentals=0),
    )(cx, aux, pz)


def body(cotangent, routes, gate_weights, hidden, galore_basis, moment, second):
    ex = lax.axis_index("expert")
    z, k = ex // 2, ex % 2
    experts = NZ * NX
    named = routes.T[None] == jnp.arange(experts, dtype=jnp.int32)[:, None, None]
    hit = jnp.any(named, axis=1)
    gate = jnp.sum(jnp.where(named, gate_weights.T[None], 0.0), axis=1)
    earlier = jnp.triu(jnp.ones((TOK, TOK), jnp.bfloat16), 1)
    before = jnp.dot(hit.astype(jnp.bfloat16), earlier, preferred_element_type=jnp.float32)
    place = jnp.where(hit, before + (CAP * k).astype(jnp.float32), -1.0)
    aux = jnp.stack([place, gate]).reshape(2, NZ, NX, TOK)
    aux = jnp.roll(aux, 7 - z, axis=1).transpose(2, 0, 1, 3)
    cx = cotangent.reshape(TOK, NX, NX, LANE).transpose(2, 0, 1, 3).reshape(NX, TOK, WIDE)
    projected = jnp.einsum(
        "jsf,jfr->jsr", hidden[0], galore_basis, preferred_element_type=jnp.float32
    ).astype(jnp.bfloat16)
    pz = projected.reshape(2, NZ, PAIR, 2, LANE).transpose(1, 0, 3, 2, 4).reshape(NZ, 2, 2 * PAIR, LANE)
    gradient = exchange(cx, aux, pz)
    new_moment = beta_one * moment + (1.0 - beta_one) * gradient
    new_second = beta_two * second + (1.0 - beta_two) * gradient * gradient
    update = (
        new_moment
        / (1.0 - beta_one**STEP)
        / (jnp.sqrt(new_second / (1.0 - beta_two**STEP)) + epsilon)
    )
    return (new_moment, new_second, update)


def solution(mesh):
    placed = (
        P(("dp", "expert"), None),
        P(("dp", "expert"), None),
        P(("dp", "expert"), None),
        P("dp", "expert", None, None),
        P("expert", None, None),
        P("expert", None, "dp"),
        P("expert", None, "dp"),
    )
    return jax.shard_map(
        body,
        mesh=mesh,
        in_specs=placed,
        out_specs=(P("expert", None, "dp"), P("expert", None, "dp"), P("expert", None, "dp")),
        check_vma=False,
    )
```

time: 234 us -> 122 us (0.52)
  waiting for transfers between devices: 135 us -> 0 us
  Pallas kernels: 0 us -> 112 us
  blocking collectives: 66.3 us -> 0 us
  between operations: 14.1 us -> 0.78 us
  matrix products: 13.9 us -> 1.94 us
  local copies, waits for them, and re-layouts: 0.8 us -> 3.91 us
    pallas_call x0 -> x1, Pallas kernels: none -> 112 us  [exchange(): pl.pallas_call(kernel, out_shape=jax.ShapeDtypeStruct((2, R, LANE), jnp.f...]
    reduce_scatter x1 -> x0, waiting for transfers between devices: 88.8 us -> none  [body(): lax.psum_scatter(partial_value, 'dp', scatter_dimension=2, tiled=True)]
    all_gather x2 -> x0, blocking collectives: 66.3 us -> none  [the longest x1 38.4 us: body(): all_routes = lax.all_gather(routes, 'expert', axis=0)]
    all_gather x1 -> x0, waiting for transfers between devices: 45.8 us -> none  [body(): gathered = lax.all_gather(cotangent, 'expert', axis=0)]
    dot_general x3 -> x1, matrix products: 12.1 us -> 0.13 us  [body(): jnp.dot(hit.astype(jnp.bfloat16), earlier, preferred_element_type=jnp.flo...]
    reshape x0 -> x5, local copies, waits for them, and re-layouts: none -> 3.87 us  [the longest x3 3.63 us: body(): cotangent.reshape(TOK, NX, NX, LANE).transpose(2, 0, 1, 3)]
  transfers between devices with their start and end apart: 2 -> 0, of which waited for: 2 -> 0; matrix products, arithmetic and copies ran while one was open for 1% -> 0% of each run, Pallas kernels for 0% -> 0%
where the time goes in v2:
time: 122 us; the launch traced here: 121 us
  Pallas kernels  112 us (92%)
  local copies, waits for them, and re-layouts  3.91 us (3%)
  other arithmetic  2.7 us (2%)
  matrix products  1.94 us (2%)
    pallas_call x1, Pallas kernels, exchange(): pl.pallas_call(kernel, out_shape=jax.ShapeDtypeStruct((2, R, LANE), jnp.f...  112 us
    reshape x3, local copies, waits for them, and re-layouts, body(): cotangent.reshape(TOK, NX, NX, LANE).transpose(2, 0, 1, 3)  3.63 us

profile of v2, /device:TPU:1, one launch (start us, length us, event | category | flops | bytes accessed | tf_op | source)
XLA Modules:
  0.0 121.3 jit_solution(10277409479301685254)
XLA Ops:
  0.6 0.0 copy-start
  0.7 0.9 fusion.7
  1.6 0.1 fusion.5
  1.7 0.8 select_reduce_fusion
  2.6 0.0 copy-done
  2.6 1.8 %fusion.2 = bf16[2,640,256]{2,1,0:T(8,128)(2,1)S(1)} fusion(bf16[2,768,256]{2,1,0:T(8,128)(2,1)} %param.11, bf16[1,2,640,768]{3,2,1,0:T(8,128)(2,1)S(1)} %copy-done), kind=kOutput, calls=%fused_computation.2 | convolution fusion | flops 503644160 | bytes 3407872 | tf_op jit(solution)/shard_map/jsf,jfr->jsr/dot_general | solution.py:297
  4.4 0.2 reshape.27
  4.6 0.1 copy.19
  4.7 1.4 %reshape.25 = bf16[128,4,4,128]{3,2,1,0:T(4,128)(2,1)S(1)} reshape(bf16[128,2048]{1,0:T(8,128)(2,1)} %param.7) | data formatting | bytes 1048576 | tf_op jit(solution)/shard_map/reshape | solution.py:296
  6.1 1.0 copy.21
  7.1 1.2 %reshape.26.cx = bf16[4,128,512]{2,1,0:T(8,128)(2,1)S(1)} reshape(bf16[4,128,4,128]{3,2,1,0:T(4,128)(2,1)} %bitcast.20) | data formatting | bytes 1048576 | tf_op jit(solution)/shard_map/reshape | solution.py:296
  8.3 0.0 copy-start.1
  8.3 0.0 copy-start.2
  8.3 111.9 %shard_map.94 = f32[2,256,128]{2,1,0:T(8,128)S(1)} custom-call(bf16[4,128,512]{2,1,0:T(8,128)(2,1)S(1)} %reshape.26.cx, f32[4,2,16,128]{3,2,1,0:T(8,128)S(1)} %fusion.10.aux, bf16[16,2,80,128]{3,2,1,0:T(8,128)(2,1)S(1)} %bitcast.19), custom_call_target="tpu_custom_call" | custom-call | flops 2700000000 | bytes 4000000 | tf_op jit(solution)/shard_map/pallas_call | solution.py:251
  120.3 0.0 copy-done.1
  120.3 0.0 copy-done.2
  120.3 1.0 add_divide_fusion
  (3 shorter events, 0.0 us)
Async XLA Ops:
  0.6 2.0 %copy-start = (bf16[1,2,640,768]{3,2,1,0:T(8,128)(2,1)S(1)}, bf16[1,2,640,768]{3,2,1,0:T(8,128)(2,1)}, u32[]{:S(2)}) copy-start(bf16[1,2,640,768]{3,2,1,0:T(8,128)(2,1)} %param.10) | copy-start | bytes 5898244
  8.3 112.0 %copy-start.1 = (f32[2,256,128]{2,1,0:T(8,128)S(1)}, f32[2,256,128]{2,1,0:T(8,128)}, u32[]{:S(2)}) copy-start(f32[2,256,128]{2,1,0:T(8,128)} %param.13) | copy-start | bytes 786436
  8.3 112.0 %copy-start.2 = (f32[2,256,128]{2,1,0:T(8,128)S(1)}, f32[2,256,128]{2,1,0:T(8,128)}, u32[]{:S(2)}) copy-start(f32[2,256,128]{2,1,0:T(8,128)} %param.12) | copy-start | bytes 786436

commit v3 on v1

v3 whole, which is shorter than its diff:
```python
import functools

import jax
import jax.numpy as jnp
from jax import lax
from jax.experimental import pallas as pl
from jax.experimental.pallas import tpu as pltpu
from jax.sharding import PartitionSpec as P

STEP = 100
MESH = pl.DeviceIdType.MESH

beta_one = 0.9
beta_two = 0.999
epsilon = 1e-08

NX = 4
NZ = 16
PLANE = NX * NX
HALF = 8
CAP = 20
PAIR = 2 * CAP
R = 256
LANE = 128
TOK = 128
WIDE = NX * LANE
FULL = 32767.0


def landed(ref, sem):
    pltpu.make_async_copy(ref, ref, sem).wait()


def kernel(
    cot, routes_in, gates_in, hidden, basis, out,
    routes, gates, cx, aux, hid, bas, pz, load_sem, prx, pg, crx, arx, tab, pt, own, rxq, rxs, txq, txs, finq, fins,
    z_send, prx_sem, c_send, a_send, c_recv, a_recv, cy_send, ax_send,
    sc_send, sa_send, sc_recv, sa_recv, p1_send, p1_recv, p2_send, p2_recv,
    q_send, s_send, q_recv, s_recv, fq_recv, fs_recv,
):
    dp = lax.axis_index("dp")
    ex = lax.axis_index("expert")
    x, y = lax.rem(dp, NX), dp // NX
    z, k = ex // 2, lax.rem(ex, 2)
    sibling = z * 2 + 1 - k
    ahead = 1 - 2 * k

    def push(src, dst, send, recv, device):
        pltpu.make_async_remote_copy(
            src_ref=src, dst_ref=dst, send_sem=send, recv_sem=recv, device_id=device, device_id_type=MESH
        ).start()

    def chip(cx_, cy_):
        return cy_ * NX + cx_

    pltpu.make_async_copy(routes_in, routes, load_sem.at[3]).start()
    pltpu.make_async_copy(gates_in, gates, load_sem.at[4]).start()
    for group in range(NX):
        for part in range(NX):
            at = (part * NX + group) * LANE
            pltpu.make_async_copy(
                cot.at[:, at : at + LANE], cx.at[group, :, part * LANE : (part + 1) * LANE], load_sem.at[0]
            ).start()
    pltpu.make_async_copy(hidden.at[0], hid, load_sem.at[1]).start()
    pltpu.make_async_copy(basis, bas, load_sem.at[2]).start()

    barrier = pltpu.get_barrier_semaphore()

    def greet(to, core):
        pl.semaphore_signal(barrier, inc=1, device_id=(to, core), device_id_type=MESH)

    def greet_z(d, carry):
        greet(dp, lax.rem(z + d, NZ) * 2 + k)
        return carry

    def greet_other(d, carry):
        greet(dp, lax.rem(z + d * ahead + NZ, NZ) * 2 + 1 - k)
        return carry

    for o in range(1, NX):
        greet(chip(lax.rem(x + o, NX), y), ex)
        greet(chip(x, lax.rem(y + o, NX)), ex)
        greet(chip(x, lax.rem(y + o, NX)), sibling)
        for near in (1, NZ - 1):
            for core in range(2):
                greet(chip(x, lax.rem(y + o, NX)), lax.rem(z + near, NZ) * 2 + core)
    greet(dp, sibling)
    lax.fori_loop(1, NZ, greet_z, 0)
    lax.fori_loop(1, HALF + 1, greet_other, 0)

    landed(routes, load_sem.at[3])
    landed(gates, load_sem.at[4])
    row = lax.broadcasted_iota(jnp.int32, (NX * NZ, TOK), 0)
    expert = lax.rem(row + (z + NZ - HALF + 1), NZ) * NX + row // NZ
    hit = jnp.zeros((NX * NZ, TOK), jnp.float32)
    gate = jnp.zeros((NX * NZ, TOK), jnp.float32)
    for n in range(routes.shape[0]):
        named = expert == routes[n : n + 1, :]
        hit = jnp.where(named, 1.0, hit)
        gate = jnp.where(named, gates[n : n + 1, :], gate)
    earlier = lax.broadcasted_iota(jnp.int32, (TOK, TOK), 0) < lax.broadcasted_iota(jnp.int32, (TOK, TOK), 1)
    before = jnp.dot(
        hit.astype(jnp.bfloat16), jnp.where(earlier, 1.0, 0.0).astype(jnp.bfloat16), preferred_element_type=jnp.float32
    )
    place = jnp.where(hit > 0.0, before + (CAP * k).astype(jnp.float32), -1.0)
    for q in range(NX):
        aux[q, 0] = place[q * NZ : (q + 1) * NZ]
        aux[q, 1] = gate[q * NZ : (q + 1) * NZ]

    landed(hid, load_sem.at[1])
    landed(bas, load_sem.at[2])
    for j in range(2):
        rows = jnp.dot(hid[j], bas[j], preferred_element_type=jnp.float32).reshape(NZ, PAIR, R)
        pz[:, j] = jnp.concatenate([rows[:, :, :LANE], rows[:, :, LANE:]], axis=1).astype(jnp.bfloat16)
    landed(cx, load_sem.at[0])

    pl.semaphore_wait(barrier, 7 * (NX - 1) + 1 + NZ - 1 + HALF)

    for o in range(1, NX):
        tx, ty = lax.rem(x + o, NX), lax.rem(y + o, NX)
        push(aux.at[ty], arx.at[x, y, k], a_send.at[o], a_recv.at[x, y], (chip(x, ty), ex))
        push(cx.at[tx], crx.at[x, y, k], c_send.at[o], c_recv.at[x, y], (chip(tx, y), ex))
    pltpu.make_async_copy(aux.at[y], arx.at[x, y, k], a_recv.at[x, y]).start()
    pltpu.make_async_copy(cx.at[x], crx.at[x, y, k], c_recv.at[x, y]).start()

    mine = pl.ds(k * 2, 2)

    def reach(d):
        i = HALF - d
        down, up = lax.rem(z - d + NZ, NZ), lax.rem(z + d, NZ)
        push(pz.at[down], prx.at[i, mine], z_send.at[i, 0], prx_sem.at[i, k], (dp, down * 2))
        if d < HALF:
            push(pz.at[up], prx.at[i, mine], z_send.at[i, 1], prx_sem.at[i, k], (dp, up * 2 + 1))

    def reached(d):
        landed(pz.at[0], z_send.at[HALF - d, 0])
        if d < HALF:
            landed(pz.at[0], z_send.at[HALF - d, 1])

    for d in range(HALF, 0, -1):
        reach(d)

    @pl.when(k == 0)
    def _():
        push(pz.at[z], prx.at[0, mine], z_send.at[0, 1], prx_sem.at[0, k], (dp, sibling))

    @pl.when(k == 1)
    def _():
        pltpu.make_async_copy(pz.at[z], prx.at[0, mine], prx_sem.at[0, k]).start()

    def share_slots(sx, sy):
        push(arx.at[sx, sy, k], arx.at[sx, sy, k], sa_send.at[sx, sy], sa_recv.at[sx, sy], (dp, sibling))

    def share_columns(sx, sy):
        push(crx.at[sx, sy, k], crx.at[sx, sy, k], sc_send.at[sx, sy], sc_recv.at[sx, sy], (dp, sibling))

    def forward(o):
        sy = lax.rem(y - o + NX, NX)
        landed(arx.at[x, sy, k], a_recv.at[x, sy])
        for t in range(1, NX):
            push(arx.at[x, sy, k], arx.at[x, sy, k], ax_send.at[o, t], a_recv.at[x, sy], (chip(lax.rem(x + t, NX), y), ex))
        share_slots(x, sy)
        sx = lax.rem(x - o + NX, NX)
        landed(crx.at[sx, y, k], c_recv.at[sx, y])
        for t in range(1, NX):
            push(crx.at[sx, y, k], crx.at[sx, y, k], cy_send.at[o, t], c_recv.at[sx, y], (chip(x, lax.rem(y + t, NX)), ex))
        share_columns(sx, y)

    def spread_y(i):
        for core in range(2):
            landed(prx.at[i, pl.ds(core * 2, 2)], prx_sem.at[i, core])
        for t in range(1, NX):
            ty = lax.rem(y + t, NX)
            push(prx.at[i, ty], pg.at[i, x, y], p1_send.at[i, t], p1_recv.at[i, y], (chip(x, ty), ex))
        pltpu.make_async_copy(prx.at[i, y], pg.at[i, x, y], p1_recv.at[i, y]).start()

    def spread_x(i):
        for sy in range(NX):
            landed(pg.at[i, x, sy], p1_recv.at[i, sy])
        for t in range(1, NX):
            push(pg.at[i, x], pg.at[i, x], p2_send.at[i, t], p2_recv.at[i, x], (chip(lax.rem(x + t, NX), y), ex))

    def receive(o, t):
        sx, sy = lax.rem(x - t + NX, NX), lax.rem(y - o + NX, NX)
        landed(arx.at[sx, sy, k], a_recv.at[sx, sy])
        share_slots(sx, sy)
        sx, sy = lax.rem(x - o + NX, NX), lax.rem(y - t + NX, NX)
        landed(crx.at[sx, sy, k], c_recv.at[sx, sy])
        share_columns(sx, sy)

    first = pl.multiple_of((1 - k) * HALF, HALF)
    slot = lax.broadcasted_iota(jnp.int32, (HALF, PAIR, 2 * TOK), 1).astype(jnp.float32)

    def rows_of(sx, sy):
        landed(arx.at[sx, sy, 1 - k], sa_recv.at[sx, sy])
        landed(crx.at[sx, sy, 1 - k], sc_recv.at[sx, sy])
        place = jnp.concatenate([arx[sx, sy, c, 0, pl.ds(first, HALF), :] for c in range(2)], axis=1)
        gate = jnp.concatenate([arx[sx, sy, c, 1, pl.ds(first, HALF), :] for c in range(2)], axis=1)
        here = slot == place[:, None, :]
        weight = jnp.sum(jnp.where(here, gate[:, None, :], 0.0), axis=2, keepdims=True)
        pick = jnp.where(here, 1.0, 0.0).reshape(HALF * PAIR, 2 * TOK).astype(jnp.bfloat16)
        rows = jnp.dot(pick, crx[sx, sy].reshape(2 * TOK, WIDE), preferred_element_type=jnp.float32)
        return rows.reshape(HALF, PAIR, WIDE) * weight

    def build(pair, carry):
        sx, sy = pair // 2, 2 * lax.rem(pair, 2)
        both = jnp.concatenate([rows_of(sx, sy), rows_of(sx, sy + 1)], axis=1)
        tab[:, pair] = both.astype(jnp.bfloat16)
        return carry

    todo = [(o, t) for o in range(NX) for t in range(1, NX)]

    def take(n):
        for _ in range(n):
            receive(*todo.pop(0))

    def more(d):
        reached(d + 3)
        reach(d)

    onward = lax.rem(z + ahead + NZ, NZ) * 2 + k

    def turn(i):
        for t in range(1, NX):
            sx = lax.rem(x + t, NX)
            landed(pg.at[i, sx], p2_recv.at[i, sx])
        got = pg[i].astype(jnp.float32).reshape(PLANE, 2, PAIR, LANE)
        for h in range(2):
            pt[i, h * LANE : (h + 1) * LANE, :] = got[:, h].reshape(PLANE * PAIR, LANE).T.astype(jnp.bfloat16)

    def block(i, b):
        table = tab[jnp.where(k == 0, HALF - 1 - i, (i + HALF - 1) % HALF), :, :, b * LANE : (b + 1) * LANE]
        return jnp.dot(pt[i], table.reshape(PLANE * PAIR, LANE), preferred_element_type=jnp.float32)

    def arrived(i, b):
        landed(rxs.at[i, b], s_recv.at[i, b])
        landed(rxq.at[i, b], q_recv.at[i, b])
        return rxq[i, b].astype(jnp.int32).astype(jnp.float32) * rxs[i, b, 0:1, :]

    def code(value, i, b):
        most = jnp.maximum(jnp.max(jnp.abs(value), axis=0, keepdims=True), 1e-33)
        txq[i, b] = jnp.round(value * (FULL / most)).astype(jnp.int32).astype(jnp.int16)
        txs[i, b] = jnp.broadcast_to(most * (1.0 / FULL), (8, LANE))

    def push_on(i, b):
        push(txs.at[i, b], rxs.at[i + 1, b], s_send.at[i, b], s_recv.at[i + 1, b], (dp, onward))
        push(txq.at[i, b], rxq.at[i + 1, b], q_send.at[i, b], q_recv.at[i + 1, b], (dp, onward))

    owner_core = y // 2
    part = lax.rem(y, 2)

    def here(b):
        return (y == b) & (owner_core == k)

    def push_owner(i, b, source, plane):
        owner = (b * NX + x, plane * 2 + owner_core)
        push(txs.at[i, b], fins.at[source, part], s_send.at[i, b], fs_recv.at[source, part], owner)
        push(txq.at[i, b], finq.at[source, part], q_send.at[i, b], fq_recv.at[source, part], owner)

    def hop(i):
        turn(i)
        for b in range(NX):
            value = block(i, b)
            if i == 0:
                code(value, 0, b)

                @pl.when(k == 0)
                def _():
                    push_on(0, b)

                @pl.when((k == 1) & here(b))
                def _():
                    pltpu.make_async_copy(txs.at[0, b], fins.at[2, part], fs_recv.at[2, part]).start()
                    pltpu.make_async_copy(txq.at[0, b], finq.at[2, part], fq_recv.at[2, part]).start()

                @pl.when((k == 1) & jnp.logical_not(here(b)))
                def _():
                    push_owner(0, b, 2, z)

            elif i == 1:
                own[...] = value

                @pl.when(k == 0)
                def _():
                    own[...] += arrived(1, b)

                code(own[...], 1, b)
                push_on(1, b)
            else:
                code(value + arrived(i, b), i, b)
                if i < HALF - 1:
                    push_on(i, b)
                else:
                    push_owner(i, b, k, lax.rem(z + ahead + NZ, NZ))

    for o in range(NX):
        forward(o)
    for i in range(HALF):
        spread_y(i)
        if i > 2:
            spread_x(i - 3)
        if i % 2:
            take(3)
    lax.fori_loop(0, 4, build, 0)
    spread_x(5)
    lax.fori_loop(4, 6, build, 0)
    spread_x(6)
    lax.fori_loop(6, 8, build, 0)
    spread_x(7)
    for i in range(HALF):
        hop(i)

    for j in range(2):
        total = None
        for core in (2, 0, 1):
            landed(fins.at[core, j], fs_recv.at[core, j])
            landed(finq.at[core, j], fq_recv.at[core, j])
            value = finq[core, j].astype(jnp.int32).astype(jnp.float32) * fins[core, j, 0:1, :]
            total = value if total is None else total + value
        out[j] = total

    for d in range(HALF, 0, -1):
        reached(d)

    @pl.when(k == 0)
    def _():
        landed(pz.at[0], z_send.at[0, 1])

    def left(i, carry):
        for t in range(1, NX):
            landed(pz.at[0, 0], p1_send.at[i, t])
            landed(pg.at[i, 0], p2_send.at[i, t])
        return carry

    lax.fori_loop(0, HALF, left, 0)

    def gone(o, carry):
        for t in range(NX):
            landed(aux.at[0], sa_send.at[o, t])
            landed(cx.at[0], sc_send.at[o, t])
        for t in range(1, NX):
            landed(aux.at[0], ax_send.at[o, t])
            landed(cx.at[0], cy_send.at[o, t])

        @pl.when(o > 0)
        def _():
            landed(aux.at[0], a_send.at[o])
            landed(cx.at[0], c_send.at[o])

        return carry

    lax.fori_loop(0, NX, gone, 0)

    def sent(i, carry):
        for b in range(NX):
            landed(txs.at[i, b], s_send.at[i, b])
            landed(txq.at[i, b], q_send.at[i, b])
        return carry

    lax.fori_loop(1, HALF, sent, 0)

    for b in range(NX):

        @pl.when((k == 0) | jnp.logical_not(here(b)))
        def _():
            landed(txs.at[0, b], s_send.at[0, b])
            landed(txq.at[0, b], q_send.at[0, b])


def exchange(cotangent, routes, gates, hidden, basis):
    dma = pltpu.SemaphoreType.DMA
    square = dma((NX, NX))
    return pl.pallas_call(
        kernel,
        out_shape=jax.ShapeDtypeStruct((2, R, LANE), jnp.float32),
        in_specs=[pl.BlockSpec(memory_space=pltpu.HBM)] * 5,
        out_specs=pl.BlockSpec(memory_space=pltpu.VMEM),
        scratch_shapes=[
            pltpu.VMEM(routes.shape, jnp.int32),
            pltpu.VMEM(gates.shape, jnp.float32),
            pltpu.VMEM((NX, TOK, WIDE), jnp.bfloat16),
            pltpu.VMEM((NX, 2, NZ, TOK), jnp.float32),
            pltpu.VMEM(hidden.shape[1:], jnp.bfloat16),
            pltpu.VMEM(basis.shape, jnp.bfloat16),
            pltpu.VMEM((NZ, 2, 2 * PAIR, LANE), jnp.bfloat16),
            dma((5,)),
            pltpu.VMEM((HALF, NX, 2 * PAIR, LANE), jnp.bfloat16),
            pltpu.VMEM((HALF, NX, NX, 2 * PAIR, LANE), jnp.bfloat16),
            pltpu.VMEM((NX, NX, 2, TOK, WIDE), jnp.bfloat16),
            pltpu.VMEM((NX, NX, 2, 2, NZ, TOK), jnp.float32),
            pltpu.VMEM((HALF, PLANE // 2, 2 * PAIR, WIDE), jnp.bfloat16),
            pltpu.VMEM((HALF, R, PLANE * PAIR), jnp.bfloat16),
            pltpu.VMEM((R, LANE), jnp.float32),
            pltpu.VMEM((HALF + 1, NX, R, LANE), jnp.int16),
            pltpu.VMEM((HALF + 1, NX, 8, LANE), jnp.float32),
            pltpu.VMEM((HALF + 1, NX, R, LANE), jnp.int16),
            pltpu.VMEM((HALF + 1, NX, 8, LANE), jnp.float32),
            pltpu.VMEM((3, 2, R, LANE), jnp.int16),
            pltpu.VMEM((3, 2, 8, LANE), jnp.float32),
            dma((HALF, 2)),
            dma((HALF, 2)),
            dma((NX,)), dma((NX,)), square, square, square, square,
            square, square, square, square,
            dma((HALF, NX)), dma((HALF, NX)), dma((HALF, NX)), dma((HALF, NX)),
            dma((HALF, NX)), dma((HALF, NX)),
            dma((HALF + 1, NX)), dma((HALF + 1, NX)),
            dma((3, 2)), dma((3, 2)),
        ],
        compiler_params=pltpu.CompilerParams(
            collective_id=0, has_side_effects=True, vmem_limit_bytes=56 * 1024 * 1024
        ),
        cost_estimate=pl.CostEstimate(flops=2_700_000_000, bytes_accessed=4_000_000, transcendentals=0),
    )(cotangent, routes, gates, hidden, basis)


def body(cotangent, routes, gate_weights, hidden, galore_basis, moment, second):
    gradient = exchange(cotangent, routes.T, gate_weights.T, hidden, galore_basis)
    new_moment = beta_one * moment + (1.0 - beta_one) * gradient
    new_second = beta_two * second + (1.0 - beta_two) * gradient * gradient
    update = (
        new_moment
        / (1.0 - beta_one**STEP)
        / (jnp.sqrt(new_second / (1.0 - beta_two**STEP)) + epsilon)
    )
    return (new_moment, new_second, update)


def solution(mesh):
    placed = (
        P(("dp", "expert"), None),
        P(("dp", "expert"), None),
        P(("dp", "expert"), None),
        P("dp", "expert", None, None),
        P("expert", None, None),
        P("expert", None, "dp"),
        P("expert", None, "dp"),
    )
    return jax.shard_map(
        body,
        mesh=mesh,
        in_specs=placed,
        out_specs=(P("expert", None, "dp"), P("expert", None, "dp"), P("expert", None, "dp")),
        check_vma=False,
    )
```

time: 234 us -> 92.4 us (0.39)
  waiting for transfers between devices: 135 us -> 0 us
  Pallas kernels: 0 us -> 89.1 us
  blocking collectives: 66.3 us -> 0 us
  matrix products: 13.9 us -> 0 us
  between operations: 14.1 us -> 0.67 us
    pallas_call x0 -> x1, Pallas kernels: none -> 89.1 us  [exchange(): pl.pallas_call(kernel, out_shape=jax.ShapeDtypeStruct((2, R, LANE), jnp.f...]
    reduce_scatter x1 -> x0, waiting for transfers between devices: 88.8 us -> none  [body(): lax.psum_scatter(partial_value, 'dp', scatter_dimension=2, tiled=True)]
    all_gather x2 -> x0, blocking collectives: 66.3 us -> none  [the longest x1 38.4 us: body(): all_routes = lax.all_gather(routes, 'expert', axis=0)]
    all_gather x1 -> x0, waiting for transfers between devices: 45.8 us -> none  [body(): gathered = lax.all_gather(cotangent, 'expert', axis=0)]
    dot_general x4 -> x0, matrix products: 13.9 us -> none  [the longest x1 8.09 us: body(): jnp.einsum('jsct,std->jscd', chosen.astype(jnp.bfloat16), gathered, prefe...]
  transfers between devices with their start and end apart: 2 -> 0, of which waited for: 2 -> 0; matrix products, arithmetic and copies ran while one was open for 1% -> 0% of each run, Pallas kernels for 0% -> 0%
where the time goes in v3:
time: 92.4 us; the launch traced here: 91.7 us
  Pallas kernels  89.1 us (96%)
  other arithmetic  1.91 us (2%)
    pallas_call x1, Pallas kernels, exchange(): pl.pallas_call(kernel, out_shape=jax.ShapeDtypeStruct((2, R, LANE), jnp.f...  89.1 us
    div x1, other arithmetic, body(): new_moment / (1.0 - beta_one ** STEP)  1.91 us

profile of v3, /device:TPU:1, one launch (start us, length us, event | category | flops | bytes accessed | tf_op | source)
XLA Modules:
  0.0 91.7 jit_solution(6379751791711740342)
XLA Ops:
  0.6 0.0 copy-start
  0.6 0.0 copy-start.1
  0.7 89.1 %shard_map.94 = f32[2,256,128]{2,1,0:T(8,128)} custom-call(bf16[128,2048]{1,0:T(8,128)(2,1)} %cot.1, s32[8,128]{1,0:T(8,128)} %bitcast.2, f32[8,128]{1,0:T(8,128)} %bitcast.3, bf16[1,2,640,768]{3,2,1,0:T(8,128)(2,1)} %hidden.1, bf16[2,768,256]{2,1,0:T(8,128)(2,1)} %basis.1), custom_call_target="tpu_custom_call" | custom-call | flops 2700000000 | bytes 4000000 | tf_op jit(solution)/shard_map/pallas_call | solution.py:373
  89.8 0.0 copy-done
  89.8 0.0 copy-done.1
  89.8 1.9 %add_divide_fusion = (f32[2,256,128]{2,1,0:T(8,128)}, f32[2,256,128]{2,1,0:T(8,128)}, f32[2,256,128]{2,1,0:T(8,128)}) fusion(f32[2,256,128]{2,1,0:T(8,128)} %shard_map.94, f32[2,256,128]{2,1,0:T(8,128)S(1)} %copy-done, f32[2,256,128]{2,1,0:T(8,128)S(1)} %copy-done.1), kind=kLoop, calls=%fused_computation.2 | loop fusion | flops 720896 | bytes 1572864 | tf_op jit(solution)/shard_map/div | solution.py:421
Async XLA Ops:
  0.6 89.1 %copy-start = (f32[2,256,128]{2,1,0:T(8,128)S(1)}, f32[2,256,128]{2,1,0:T(8,128)}, u32[]{:S(2)}) copy-start(f32[2,256,128]{2,1,0:T(8,128)} %param.13) | copy-start | bytes 786436
  0.6 89.1 %copy-start.1 = (f32[2,256,128]{2,1,0:T(8,128)S(1)}, f32[2,256,128]{2,1,0:T(8,128)}, u32[]{:S(2)}) copy-start(f32[2,256,128]{2,1,0:T(8,128)} %param.12) | copy-start | bytes 786436

commit v4 on v3

--- a/solution.py
+++ b/solution.py
@@ -53,6 +53,30 @@
     def chip(cx_, cy_):
         return cy_ * NX + cx_
 
+    barrier = pltpu.get_barrier_semaphore()
+
+    def greet(to, core):
+        pl.semaphore_signal(barrier, inc=1, device_id=(to, core), device_id_type=MESH)
+
+    def greet_z(d, carry):
+        greet(dp, lax.rem(z + d, NZ) * 2 + k)
+        return carry
+
+    def greet_other(d, carry):
+        greet(dp, lax.rem(z + d * ahead + NZ, NZ) * 2 + 1 - k)
+        return carry
+
+    lax.fori_loop(1, NZ, greet_z, 0)
+    lax.fori_loop(1, HALF + 1, greet_other, 0)
+    for o in range(1, NX):
+        greet(chip(lax.rem(x + o, NX), y), ex)
+        greet(chip(x, lax.rem(y + o, NX)), ex)
+        greet(chip(x, lax.rem(y + o, NX)), sibling)
+        for near in (1, NZ - 1):
+            for core in range(2):
+                greet(chip(x, lax.rem(y + o, NX)), lax.rem(z + near, NZ) * 2 + core)
+    greet(dp, sibling)
+
     pltpu.make_async_copy(routes_in, routes, load_sem.at[3]).start()
     pltpu.make_async_copy(gates_in, gates, load_sem.at[4]).start()
     for group in range(NX):
@@ -63,30 +87,6 @@
             ).start()
     pltpu.make_async_copy(hidden.at[0], hid, load_sem.at[1]).start()
     pltpu.make_async_copy(basis, bas, load_sem.at[2]).start()
-
-    barrier = pltpu.get_barrier_semaphore()
-
-    def greet(to, core):
-        pl.semaphore_signal(barrier, inc=1, device_id=(to, core), device_id_type=MESH)
-
-    def greet_z(d, carry):
-        greet(dp, lax.rem(z + d, NZ) * 2 + k)
-        return carry
-
-    def greet_other(d, carry):
-        greet(dp, lax.rem(z + d * ahead + NZ, NZ) * 2 + 1 - k)
-        return carry
-
-    for o in range(1, NX):
-        greet(chip(lax.rem(x + o, NX), y), ex)
-        greet(chip(x, lax.rem(y + o, NX)), ex)
-        greet(chip(x, lax.rem(y + o, NX)), sibling)
-        for near in (1, NZ - 1):
-            for core in range(2):
-                greet(chip(x, lax.rem(y + o, NX)), lax.rem(z + near, NZ) * 2 + core)
-    greet(dp, sibling)
-    lax.fori_loop(1, NZ, greet_z, 0)
-    lax.fori_loop(1, HALF + 1, greet_other, 0)
 
     landed(routes, load_sem.at[3])
     landed(gates, load_sem.at[4])
@@ -162,7 +162,7 @@
         share_slots(x, sy)
         sx = lax.rem(x - o + NX, NX)
         landed(crx.at[sx, y, k], c_recv.at[sx, y])
-        for t in range(1, NX):
+        for t in (1, NX - 1):
             push(crx.at[sx, y, k], crx.at[sx, y, k], cy_send.at[o, t], c_recv.at[sx, y], (chip(x, lax.rem(y + t, NX)), ex))
         share_columns(sx, y)
 
@@ -186,6 +186,9 @@
         share_slots(sx, sy)
         sx, sy = lax.rem(x - o + NX, NX), lax.rem(y - t + NX, NX)
         landed(crx.at[sx, sy, k], c_recv.at[sx, sy])
+        if t == (1 if o % 2 == 0 else NX - 1):
+            over = chip(x, lax.rem(y + t, NX))
+            push(crx.at[sx, sy, k], crx.at[sx, sy, k], cy_send.at[o, 2], c_recv.at[sx, sy], (over, ex))
         share_columns(sx, sy)
 
     first = pl.multiple_of((1 - k) * HALF, HALF)
@@ -208,7 +211,10 @@
         tab[:, pair] = both.astype(jnp.bfloat16)
         return carry
 
-    todo = [(o, t) for o in range(NX) for t in range(1, NX)]
+    todo = [(0, 1), (0, 3)]
+    for o in range(1, NX):
+        todo += [(o, 1), (o, 3), (o - 1, 2)]
+    todo.append((NX - 1, 2))
 
     def take(n):
         for _ in range(n):
@@ -260,7 +266,9 @@
     def hop(i):
         turn(i)
         for b in range(NX):
-            value = block(i, b)
+            own[b] = block(i, b)
+        for b in range(NX):
+            value = own[b]
             if i == 0:
                 code(value, 0, b)
 
@@ -278,13 +286,11 @@
                     push_owner(0, b, 2, z)
 
             elif i == 1:
-                own[...] = value
-
                 @pl.when(k == 0)
                 def _():
-                    own[...] += arrived(1, b)
-
-                code(own[...], 1, b)
+                    own[b] += arrived(1, b)
+
+                code(own[b], 1, b)
                 push_on(1, b)
             else:
                 code(value + arrived(i, b), i, b)
@@ -293,22 +299,41 @@
                 else:
                     push_owner(i, b, k, lax.rem(z + ahead + NZ, NZ))
 
-    for o in range(NX):
-        forward(o)
-    for i in range(HALF):
-        spread_y(i)
-        if i > 2:
-            spread_x(i - 3)
-        if i % 2:
-            take(3)
+    forward(0)
+    forward(1)
+    forward(2)
+    forward(3)
+    take(2)
+    spread_y(0)
+    take(3)
+    spread_y(1)
+    take(3)
+    spread_x(0)
+    spread_x(1)
+    take(3)
+    spread_y(2)
+    spread_y(3)
+    spread_y(4)
+    take(1)
+    spread_x(2)
+    spread_y(5)
+    spread_x(3)
+    spread_y(6)
+    spread_x(4)
+    spread_y(7)
     lax.fori_loop(0, 4, build, 0)
     spread_x(5)
-    lax.fori_loop(4, 6, build, 0)
+    lax.fori_loop(4, 8, build, 0)
+    hop(0)
     spread_x(6)
-    lax.fori_loop(6, 8, build, 0)
+    hop(1)
     spread_x(7)
-    for i in range(HALF):
-        hop(i)
+    hop(2)
+    hop(3)
+    hop(4)
+    hop(5)
+    hop(6)
+    hop(7)
 
     for j in range(2):
         total = None
@@ -390,7 +415,7 @@
             pltpu.VMEM((NX, NX, 2, 2, NZ, TOK), jnp.float32),
             pltpu.VMEM((HALF, PLANE // 2, 2 * PAIR, WIDE), jnp.bfloat16),
             pltpu.VMEM((HALF, R, PLANE * PAIR), jnp.bfloat16),
-            pltpu.VMEM((R, LANE), jnp.float32),
+            pltpu.VMEM((NX, R, LANE), jnp.float32),
             pltpu.VMEM((HALF + 1, NX, R, LANE), jnp.int16),
             pltpu.VMEM((HALF + 1, NX, 8, LANE), jnp.float32),
             pltpu.VMEM((HALF + 1, NX, R, LANE), jnp.int16),

time: 92.4 us -> 90.6 us (0.981)
  Pallas kernels: 89.1 us -> 87.7 us
    pallas_call x1, Pallas kernels: 89.1 us -> 87.7 us  [exchange(): pl.pallas_call(kernel, out_shape=jax.ShapeDtypeStruct((2, R, LANE), jnp.f...]
where the time goes in v4:
time: 90.6 us; the launch traced here: 90.3 us
  Pallas kernels  87.7 us (97%)
  other arithmetic  1.91 us (2%)
    pallas_call x1, Pallas kernels, exchange(): pl.pallas_call(kernel, out_shape=jax.ShapeDtypeStruct((2, R, LANE), jnp.f...  87.7 us
    div x1, other arithmetic, body(): new_moment / (1.0 - beta_one ** STEP)  1.91 us

profile of v4, /device:TPU:1, one launch (start us, length us, event | category | flops | bytes accessed | tf_op | source)
XLA Modules:
  0.0 90.3 jit_solution(2081116168609662679)
XLA Ops:
  0.6 0.0 copy-start
  0.6 0.0 copy-start.1
  0.7 87.7 %shard_map.94 = f32[2,256,128]{2,1,0:T(8,128)} custom-call(bf16[128,2048]{1,0:T(8,128)(2,1)} %cot.1, s32[8,128]{1,0:T(8,128)} %bitcast.2, f32[8,128]{1,0:T(8,128)} %bitcast.3, bf16[1,2,640,768]{3,2,1,0:T(8,128)(2,1)} %hidden.1, bf16[2,768,256]{2,1,0:T(8,128)(2,1)} %basis.1), custom_call_target="tpu_custom_call" | custom-call | flops 2700000000 | bytes 4000000 | tf_op jit(solution)/shard_map/pallas_call | solution.py:398
  88.3 0.0 copy-done
  88.3 0.0 copy-done.1
  88.4 1.9 %add_divide_fusion = (f32[2,256,128]{2,1,0:T(8,128)}, f32[2,256,128]{2,1,0:T(8,128)}, f32[2,256,128]{2,1,0:T(8,128)}) fusion(f32[2,256,128]{2,1,0:T(8,128)} %shard_map.94, f32[2,256,128]{2,1,0:T(8,128)S(1)} %copy-done, f32[2,256,128]{2,1,0:T(8,128)S(1)} %copy-done.1), kind=kLoop, calls=%fused_computation.2 | loop fusion | flops 720896 | bytes 1572864 | tf_op jit(solution)/shard_map/div | solution.py:446
Async XLA Ops:
  0.6 87.7 %copy-start = (f32[2,256,128]{2,1,0:T(8,128)S(1)}, f32[2,256,128]{2,1,0:T(8,128)}, u32[]{:S(2)}) copy-start(f32[2,256,128]{2,1,0:T(8,128)} %param.13) | copy-start | bytes 786436
  0.6 87.7 %copy-start.1 = (f32[2,256,128]{2,1,0:T(8,128)S(1)}, f32[2,256,128]{2,1,0:T(8,128)}, u32[]{:S(2)}) copy-start(f32[2,256,128]{2,1,0:T(8,128)} %param.12) | copy-start | bytes 786436

commit v5 on v4

--- a/solution.py
+++ b/solution.py
@@ -53,6 +53,11 @@
     def chip(cx_, cy_):
         return cy_ * NX + cx_
 
+    pltpu.make_async_copy(hidden.at[0], hid, load_sem.at[1]).start()
+    pltpu.make_async_copy(basis, bas, load_sem.at[2]).start()
+    pltpu.make_async_copy(routes_in, routes, load_sem.at[3]).start()
+    pltpu.make_async_copy(gates_in, gates, load_sem.at[4]).start()
+
     barrier = pltpu.get_barrier_semaphore()
 
     def greet(to, core):
@@ -77,16 +82,12 @@
                 greet(chip(x, lax.rem(y + o, NX)), lax.rem(z + near, NZ) * 2 + core)
     greet(dp, sibling)
 
-    pltpu.make_async_copy(routes_in, routes, load_sem.at[3]).start()
-    pltpu.make_async_copy(gates_in, gates, load_sem.at[4]).start()
     for group in range(NX):
         for part in range(NX):
             at = (part * NX + group) * LANE
             pltpu.make_async_copy(
                 cot.at[:, at : at + LANE], cx.at[group, :, part * LANE : (part + 1) * LANE], load_sem.at[0]
             ).start()
-    pltpu.make_async_copy(hidden.at[0], hid, load_sem.at[1]).start()
-    pltpu.make_async_copy(basis, bas, load_sem.at[2]).start()
 
     landed(routes, load_sem.at[3])
     landed(gates, load_sem.at[4])

time: 90.6 us -> 89.9 us (level)
  no operation moved by 1% of the time
where the time goes in v5:
time: 89.9 us; the launch traced here: 89.7 us
  Pallas kernels  87.1 us (97%)
  other arithmetic  1.91 us (2%)
    pallas_call x1, Pallas kernels, exchange(): pl.pallas_call(kernel, out_shape=jax.ShapeDtypeStruct((2, R, LANE), jnp.f...  87.1 us
    div x1, other arithmetic, body(): new_moment / (1.0 - beta_one ** STEP)  1.91 us

profile of v5, /device:TPU:1, one launch (start us, length us, event | category | flops | bytes accessed | tf_op | source)
XLA Modules:
  0.0 89.7 jit_solution(8813448771390400451)
XLA Ops:
  0.6 0.0 copy-start
  0.6 0.0 copy-start.1
  0.7 87.1 %shard_map.94 = f32[2,256,128]{2,1,0:T(8,128)} custom-call(bf16[128,2048]{1,0:T(8,128)(2,1)} %cot.1, s32[8,128]{1,0:T(8,128)} %bitcast.2, f32[8,128]{1,0:T(8,128)} %bitcast.3, bf16[1,2,640,768]{3,2,1,0:T(8,128)(2,1)} %hidden.1, bf16[2,768,256]{2,1,0:T(8,128)(2,1)} %basis.1), custom_call_target="tpu_custom_call" | custom-call | flops 2700000000 | bytes 4000000 | tf_op jit(solution)/shard_map/pallas_call | solution.py:399
  87.7 0.0 copy-done
  87.7 0.0 copy-done.1
  87.7 1.9 %add_divide_fusion = (f32[2,256,128]{2,1,0:T(8,128)}, f32[2,256,128]{2,1,0:T(8,128)}, f32[2,256,128]{2,1,0:T(8,128)}) fusion(f32[2,256,128]{2,1,0:T(8,128)} %shard_map.94, f32[2,256,128]{2,1,0:T(8,128)S(1)} %copy-done, f32[2,256,128]{2,1,0:T(8,128)S(1)} %copy-done.1), kind=kLoop, calls=%fused_computation.2 | loop fusion | flops 720896 | bytes 1572864 | tf_op jit(solution)/shard_map/div | solution.py:447
Async XLA Ops:
  0.6 87.1 %copy-start = (f32[2,256,128]{2,1,0:T(8,128)S(1)}, f32[2,256,128]{2,1,0:T(8,128)}, u32[]{:S(2)}) copy-start(f32[2,256,128]{2,1,0:T(8,128)} %param.13) | copy-start | bytes 786436
  0.6 87.1 %copy-start.1 = (f32[2,256,128]{2,1,0:T(8,128)S(1)}, f32[2,256,128]{2,1,0:T(8,128)}, u32[]{:S(2)}) copy-start(f32[2,256,128]{2,1,0:T(8,128)} %param.12) | copy-start | bytes 786436
